TPU v7x, 256 devices: a whole 4x4x8 slice. The times are simulated.
256 devices in a mesh: group: 16 (over y, z_lo, core), tensor: 16 (over z_hi, x).
Axes of the slice: x: 4, y: 4, z: 8 (z_hi: 4, z_lo: 2; z = z_hi * 2 + z_lo), core: 2. Of those that a mesh axis runs over, the one named last changes fastest.
Arguments:
- queries: bfloat16 [2048, 8192], P('group', 'tensor'), may hold values from -70 to 70
- keys_new: bfloat16 [2048, 2048], P('group', 'tensor'), may hold values from -6 to 6, as said below
- values_new: bfloat16 [2048, 2048], P('group', 'tensor'), may hold values from -6 to 6, as said below
- cache_keys: bfloat16 [64, 16, 512, 128], P('group', 'tensor'), may hold values from -6 to 6, as said below
- cache_values: bfloat16 [64, 16, 512, 128], P('group', 'tensor'), may hold values from -6 to 6, as said below
- cache_len: int32 [64], P('group'), may hold values from 128 to 512, as said below
- accepted: int32 [64], P('group'), may hold values from 1 to 32, as said below
- entering: bfloat16 [2048, 8192], P('group', 'tensor'), may hold values from -6 to 6
- low_feature: bfloat16 [2048, 8192], P('group', 'tensor'), may hold values from -6 to 6
- mid_feature: bfloat16 [2048, 8192], P('group', 'tensor'), may hold values from -6 to 6
- out_proj: bfloat16 [8192, 8192], P('tensor'), may hold values from -0.0625 to 0.0625
- join_weight: bfloat16 [3, 8192, 4096], P(None, 'tensor', 'group'), may hold values from -0.0390625 to 0.0390625
- teacher: bfloat16 [2048, 4096], P('group'), may hold values from -6 to 6
Outputs:
- high_feature: bfloat16 [2048, 8192], P('group', 'tensor')
- draft_grad: float32 [3, 8192, 4096], P(None, 'tensor', 'group')
Inputs may be any that keep to these rules, and one draw needn't show every extreme that they name: `cache_len`: the first sequence of every group fills all 512 slots. `accepted`: the last sequence accepts all 32 tokens. `cache_keys`: entries t and u of the second dimension are equal where t * 8 // 16 equals u * 8 // 16. `cache_values`: entries t and u of the second dimension are equal where t * 8 // 16 equals u * 8 // 16. `keys_new`: column blocks t and u of 128 columns are equal where t * 8 // 16 equals u * 8 // 16. `values_new`: column blocks t and u of 128 columns are equal where t * 8 // 16 equals u * 8 // 16.
All inputs are finite; a program needn't handle non-finite values.
Results may differ from a plain program's by a relative error of at most 0.0065.
Values may be sent and summed in bfloat16 or wider, within the bound.
A program may use at most 128 MiB of HBM per device.

v0:
```python
import jax
import jax.numpy as jnp
from jax import lax
from jax.sharding import PartitionSpec as P


def attend(query, key_new, value_new, cache_keys, cache_values, cache_len):
    scale = query.shape[-1] ** (-0.5)
    s_cache = (
        jnp.einsum("spkhe,skle->skhpl", query, cache_keys, preferred_element_type=jnp.float32)
        * scale
    )
    s_new = (
        jnp.einsum("spkhe,sqke->skhpq", query, key_new, preferred_element_type=jnp.float32) * scale
    )
    slots = jnp.arange(cache_keys.shape[2], dtype=jnp.int32)
    filled = slots[None, :] < cache_len[:, None]
    s_cache = jnp.where(filled[:, None, None, None, :], s_cache, -jnp.inf)
    places = jnp.arange(query.shape[1], dtype=jnp.int32)
    causal = places[None, :] <= places[:, None]
    s_new = jnp.where(causal, s_new, -jnp.inf)
    top = jnp.maximum(jnp.max(s_cache, axis=-1), jnp.max(s_new, axis=-1))
    p_cache = jnp.exp(s_cache - top[..., None])
    p_new = jnp.exp(s_new - top[..., None])
    total = jnp.sum(p_cache, axis=-1) + jnp.sum(p_new, axis=-1)
    mixed = jnp.einsum(
        "skhpl,skle->skhpe",
        p_cache.astype(jnp.bfloat16),
        cache_values,
        preferred_element_type=jnp.float32,
    )
    mixed = mixed + jnp.einsum(
        "skhpq,sqke->skhpe",
        p_new.astype(jnp.bfloat16),
        value_new,
        preferred_element_type=jnp.float32,
    )
    result = (mixed / total[..., None]).astype(jnp.bfloat16)
    return result.transpose(0, 3, 1, 2, 4)


def shards(
    queries,
    keys_new,
    values_new,
    cache_keys,
    cache_values,
    cache_len,
    accepted,
    entering,
    low_feature,
    mid_feature,
    out_proj,
    join_weight,
    teacher,
):
    seqs = cache_len.shape[0]
    kv_local = cache_keys.shape[1]
    depth = cache_keys.shape[3]
    rows = keys_new.shape[0]
    places = rows // seqs
    per_kv = queries.shape[1] // (kv_local * depth)
    query_s = queries.reshape(seqs, places, kv_local, per_kv, depth)
    key_s = keys_new.reshape(seqs, places, kv_local, depth)
    value_s = values_new.reshape(seqs, places, kv_local, depth)
    attended = attend(query_s, key_s, value_s, cache_keys, cache_values, cache_len).reshape(
        rows, queries.shape[1]
    )
    partial_value = jnp.dot(attended, out_proj, preferred_element_type=jnp.float32)
    projected = lax.psum_scatter(partial_value, "tensor", scatter_dimension=1, tiled=True)
    high_feature = (entering.astype(jnp.float32) + projected).astype(jnp.bfloat16)
    features = jnp.concatenate([low_feature, mid_feature, high_feature], axis=1)
    local_weight = join_weight.reshape(-1, join_weight.shape[2])
    gathered = lax.all_gather(features, "group", axis=0, tiled=True)
    joined_part = jnp.dot(
        features,
        lax.all_gather(local_weight, "group", axis=1, tiled=True),
        preferred_element_type=jnp.float32,
    )
    place = jnp.arange(rows, dtype=jnp.int32) % places
    live = place < jnp.repeat(accepted, places)
    scale = seqs / jnp.sum(accepted.astype(jnp.float32))
    joined = lax.psum(joined_part, "tensor")
    error = (joined - teacher.astype(jnp.float32)) * scale
    error = jnp.where(live[:, None], error, jnp.zeros_like(error)).astype(jnp.bfloat16)
    error_cols = lax.all_to_all(error, "group", split_axis=1, concat_axis=0, tiled=True)
    draft_grad = lax.dot_general(
        gathered, error_cols, (((0,), (0,)), ((), ())), preferred_element_type=jnp.float32
    )
    return (high_feature, draft_grad.reshape(join_weight.shape))


def solution(mesh):
    return jax.shard_map(
        shards,
        mesh=mesh,
        in_specs=(
            P("group", "tensor"),
            P("group", "tensor"),
            P("group", "tensor"),
            P("group", "tensor", None, None),
            P("group", "tensor", None, None),
            P("group"),
            P("group"),
            P("group", "tensor"),
            P("group", "tensor"),
            P("group", "tensor"),
            P("tensor", None),
            P(None, "tensor", "group"),
            P("group", None),
        ),
        out_specs=(P("group", "tensor"), P(None, "tensor", "group")),
        check_vma=False,
    )
```

profile of v0, /device:TPU:32, one launch (start us, length us, event | category | flops | bytes accessed | tf_op | source)
XLA Modules:
  0.0 405.4 jit_solution(14974270197257214608)
XLA Ops:
  8.0 0.0 copy-start
  8.0 0.0 copy-start.7
  8.0 0.0 reduce-scatter.2.cloned.1.call-start
  8.1 0.8 iota_compare_fusion.1
  8.9 0.9 reshape.122
  9.8 1.1 fusion.29
  10.9 0.0 copy-done
  10.9 0.4 fusion.28
  11.3 0.1 fusion.16
  11.4 0.3 fusion.8
  11.7 1.4 fusion.11
  13.1 0.0 copy-done.7
  13.1 0.3 fusion.7
  13.4 0.1 copy.29
  13.5 6.6 %fusion.20 = f32[128,8192]{1,0:T(8,128)} fusion(bf16[512,8192]{1,0:T(8,128)(2,1)} %param.23, bf16[16,8,4,128]{3,2,1,0:T(4,128)(2,1)S(1)} %bitcast.77), kind=kOutput, calls=%fused_computation.27 | convolution fusion | flops 1073741824 | bytes 12713984 | tf_op jit(solution)/shard_map/dot_general | solution.py:69
  20.1 0.0 copy-start.3
  20.1 0.0 reduce-scatter.2.cloned.1.call-update
  20.1 0.0 all-gather.5.cloned.1.call-start
  20.1 0.5 all-gather.5.cloned.1.call-update
  20.7 0.0 all-reduce.2.cloned.1.call-start
  20.7 145.5 %reduce-scatter.2.cloned.1.call-done = f32[128,512]{1,0:T(8,128)} async-done(((f32[128,8192]{1,0:T(8,128)}), f32[128,512]{1,0:T(8,128)}) %reduce-scatter.2.cloned.1.call-update) | async-done | bytes 262160 | tf_op jit(solution)/shard_map/reduce_scatter | solution.py:70
  166.2 0.0 copy-done.5
  166.2 1.0 add_convert_fusion
  167.2 0.0 copy-start.1
  167.2 0.0 copy-start.6
  167.2 0.0 copy-start.2
  167.2 0.0 all-gather.5.cloned.1.call-done
  167.2 0.0 copy-done.3
  167.3 0.0 copy-done.4
  167.3 7.8 %fusion.27 = f32[128,4096]{1,0:T(8,128)} fusion(bf16[1536,4096]{1,0:T(8,128)(2,1)} %all-gather.5.cloned.1.call-done, bf16[128,512]{1,0:T(8,128)(2,1)S(1)} %add_convert_fusion, bf16[128,512]{1,0:T(8,128)(2,1)S(1)} %copy-done.3, bf16[128,512]{1,0:T(8,128)(2,1)S(1)} %copy-done.4), kind=kOutput, calls=%fused_computation.38 | convolution fusion | flops 1611792384 | bytes 15073280 | tf_op jit(solution)/shard_map/dot_general | solution.py:75
  175.1 0.0 all-reduce.2.cloned.1.call-update
  175.1 0.0 all-gather.3.cloned.1.call-start
  175.1 0.0 copy-done.1
  175.1 0.8 pad_maximum_fusion
  176.0 0.0 all-gather.3.cloned.1.call-update
  176.0 0.0 copy-done.6
  176.0 0.1 broadcast_in_dim.47
  176.1 0.1 reshape.129
  176.2 0.6 convert_reduce_fusion
  177.5 189.6 %all-reduce.2.cloned.1.call-done = f32[128,4096]{1,0:T(8,128)} async-done(((f32[128,4096]{1,0:T(8,128)}), f32[128,4096]{1,0:T(8,128)}) %all-reduce.2.cloned.1.call-update) | async-done | bytes 2097168 | tf_op jit(solution)/shard_map/psum | solution.py:83
  367.1 0.0 copy-done.2
  367.1 1.9 select_convert_fusion
  369.0 1.1 copy.52
  370.1 6.8 %all-to-all-start = ((bf16[128,16,256]{2,0,1:T(8,128)(2,1)}), bf16[128,16,256]{2,0,1:T(8,128)(2,1)S(1)}, u32[]{:S(2)}, u32[]{:S(2)}) async-start(bf16[128,16,256]{2,0,1:T(8,128)(2,1)} %bitcast.71), calls=%async_computation.1 | async-start | bytes 2097152 | tf_op jit(solution)/shard_map/all_to_all | solution.py:86
  376.9 0.0 all-gather.3.cloned.1.call-done
  376.9 8.7 %copy.30 = bf16[1536,2048]{1,0:T(8,128)(2,1)} copy(bf16[1536,2048]{0,1:T(8,128)(2,1)} %bitcast.72) | data formatting | bytes 12582912 | tf_op jit(solution)/shard_map/dot_general | solution.py:87
  385.6 6.7 %all-to-all-done = bf16[128,16,256]{2,0,1:T(8,128)(2,1)S(1)} async-done(((bf16[128,16,256]{2,0,1:T(8,128)(2,1)}), bf16[128,16,256]{2,0,1:T(8,128)(2,1)S(1)}, u32[]{:S(2)}, u32[]{:S(2)}) %all-to-all-start) | async-done | bytes 1048608 | tf_op jit(solution)/shard_map/all_to_all | solution.py:86
  392.2 5.7 %fusion.30 = f32[3,512,256]{2,1,0:T(8,128)} fusion(bf16[3,512,2048]{2,1,0:T(8,128)(2,1)} %bitcast.73, bf16[2048,256,1]{1,0,2:T(8,128)(2,1)S(1)} %bitcast.75), kind=kOutput, calls=%fused_computation.41 | convolution fusion | flops 1610612736 | bytes 8912896 | tf_op jit(solution)/shard_map/dot_general | solution.py:87
  (6 shorter events, 0.0 us)
Async XLA Ops:
  8.0 2.9 copy-start
  8.0 5.1 %copy-start.7 = (bf16[128,128]{1,0:T(8,128)(2,1)S(1)}, bf16[128,128]{1,0:T(8,128)(2,1)}, u32[]{:S(2)}) copy-start(bf16[128,128]{1,0:T(8,128)(2,1)} %param.15) | copy-start | bytes 98308
  8.0 158.2 %reduce-scatter.2.cloned.1.call-start = ((), (), s32[]{:S(2)}) async-start(), calls=%async_computation.2 | async-start | bytes 4456448 | tf_op jit(solution)/shard_map/reduce_scatter | solution.py:70
  20.1 146.1 %copy-start.5 = (bf16[128,512]{1,0:T(8,128)(2,1)S(1)}, bf16[128,512]{1,0:T(8,128)(2,1)}, u32[]{:S(2)}) copy-start(bf16[128,512]{1,0:T(8,128)(2,1)} %param.20) | copy-start | bytes 393220
  20.1 147.2 %copy-start.3 = (bf16[128,512]{1,0:T(8,128)(2,1)S(1)}, bf16[128,512]{1,0:T(8,128)(2,1)}, u32[]{:S(2)}) copy-start(bf16[128,512]{1,0:T(8,128)(2,1)} %param.22) | copy-start | bytes 393220
  20.1 147.2 %copy-start.4 = (bf16[128,512]{1,0:T(8,128)(2,1)S(1)}, bf16[128,512]{1,0:T(8,128)(2,1)}, u32[]{:S(2)}) copy-start(bf16[128,512]{1,0:T(8,128)(2,1)} %param.21) | copy-start | bytes 393220
  20.1 147.1 %all-gather.5.cloned.1.call-start = ((), (), s32[]{:S(2)}) async-start(), calls=%async_computation.4 | async-start | bytes 13369344 | tf_op jit(solution)/shard_map/all_gather | solution.py:77
  20.7 346.4 %all-reduce.2.cloned.1.call-start = ((), (), s32[]{:S(2)}) async-start(), calls=%async_computation.5 | async-start | bytes 4194304 | tf_op jit(solution)/shard_map/psum | solution.py:83
  167.2 8.0 %copy-start.1 = (bf16[128,512]{1,0:T(8,128)(2,1)}, bf16[128,512]{1,0:T(8,128)(2,1)S(1)}, u32[]{:S(2)}) copy-start(bf16[128,512]{1,0:T(8,128)(2,1)S(1)} %add_convert_fusion) | copy-start | bytes 393220
  167.2 8.8 %copy-start.6 = (s32[4]{0:T(128)S(1)}, s32[4]{0:T(128)}, u32[]{:S(2)}) copy-start(s32[4]{0:T(128)} %param.19) | copy-start | bytes 52
  167.2 199.9 %copy-start.2 = (bf16[128,4096]{1,0:T(8,128)(2,1)S(1)}, bf16[128,4096]{1,0:T(8,128)(2,1)}, u32[]{:S(2)}) copy-start(bf16[128,4096]{1,0:T(8,128)(2,1)} %param.25) | copy-start | bytes 3145732
  175.1 201.8 %all-gather.3.cloned.1.call-start = ((), (), s32[]{:S(2)}) async-start(), calls=%async_computation.3 | async-start | bytes 6684672 | tf_op jit(solution)/shard_map/all_gather | solution.py:74
  370.1 22.1 %all-to-all-start = ((bf16[128,16,256]{2,0,1:T(8,128)(2,1)}), bf16[128,16,256]{2,0,1:T(8,128)(2,1)S(1)}, u32[]{:S(2)}, u32[]{:S(2)}) async-start(bf16[128,16,256]{2,0,1:T(8,128)(2,1)} %bitcast.71), calls=%async_computation.1 | async-start | bytes 2097152 | tf_op jit(solution)/shard_map/all_to_all | solution.py:86
Sparse Core Ops, SparseCore 0:
  20.2 145.9 reduce-scatter.1
  175.2 191.8 all-reduce.1
Sparse Core Ops, SparseCore 1:
  22.5 98.0 all-gather.4
  177.6 55.0 all-gather.2
where the time goes:
time: 408 us; the launch traced here: 405 us
  waiting for transfers between devices  342 us (84%)
  matrix products  23.2 us (6%)
  between operations  16.3 us (4%)
  local copies, waits for them, and re-layouts  11 us (3%)
  starting transfers between devices  6.96 us (2%)
  other arithmetic  5.55 us (1%)
    psum x1, waiting for transfers between devices, shards(): joined = lax.psum(joined_part, 'tensor')  190 us
    reduce_scatter x1, waiting for transfers between devices, shards(): lax.psum_scatter(partial_value, 'tensor', scatter_dimension=1, tiled=True)  145 us
    dot_general x1, local copies, waits for them, and re-layouts, shards(): lax.dot_general(gathered, error_cols, (((0,), (0,)), ((), ())), preferred...  8.67 us
  transfers between devices with their start and end apart: 5, of which 3 were waited for; matrix products, arithmetic and copies ran while one was open for 4% of the time, Pallas kernels for 0%

commit v1 on v0

v1 whole, which is shorter than its diff:
```python
import jax
import jax.numpy as jnp
from jax import lax
from jax.experimental import pallas as pl
from jax.experimental.pallas import tpu as pltpu
from jax.sharding import PartitionSpec as P

MESH = pl.DeviceIdType.MESH
F32 = jnp.float32
BF16 = jnp.bfloat16
COPIES = 160
LOADS = 96
OTHER = {1: 3, 3: 1}


def xor4(v, k):
    return ((v // 2 + k // 2) % 2) * 2 + (v % 2 + k % 2) % 2


def dot(a, b):
    return jnp.dot(a, b, preferred_element_type=F32)


def dot_nt(a, b):
    return lax.dot_general(a, b, (((1,), (1,)), ((), ())), preferred_element_type=F32)


class Part:
    def __init__(self, bufs, x_first, a, a2):
        self.s1, self.r1, self.k1, self.s2, self.r2, self.k2, self.s3, self.r3, self.s4, self.r4 = bufs
        self.x_first, self.a, self.b, self.a2, self.b2 = x_first, a, OTHER[a], a2, OTHER[a2]
        self.order1 = (0, self.b, a, 2)
        self.order2 = (0, self.b2, a2, 2)

    def place(self, kz, kx):
        first, second = (kx, kz) if self.x_first else (kz, kx)
        return self.order1.index(first), self.order2.index(second)

    def store(self, kz, kx, columns, value):
        first, second = self.place(kz, kx)
        if first >= 2:
            self.s1[first - 2, second, :, columns] = value.astype(BF16)
        else:
            self.k1[first, second, :, columns] = value


def part_shapes(rows, width):
    return [
        pltpu.VMEM((2, 4, rows, width), BF16),
        pltpu.VMEM((2, 4, rows, width), BF16),
        pltpu.VMEM((2, 4, rows, width), F32),
        pltpu.VMEM((4, rows, width), BF16),
        pltpu.VMEM((4, rows, width), BF16),
        pltpu.VMEM((2, rows, width), F32),
        pltpu.VMEM((2, rows, width), BF16),
        pltpu.VMEM((2, rows, width), BF16),
        pltpu.VMEM((rows, width), BF16),
        pltpu.VMEM((rows, width), BF16),
    ]


PARTS = ((True, 1, 1), (True, 3, 3), (False, 1, 1), (False, 3, 3))
ROW_PARTS = ((0, 48), (48, 48), (96, 16), (112, 16))
COL_PARTS = ((0, 384), (384, 384), (768, 128), (896, 128))
KX_ORDER = (2, 1, 3, 0)
KZ_ORDER = (2, 1, 3, 0)


def kernel(
    q_h, kn_h, vn_h, ck_h, cv_h, clen, acc, ent_h, low_h, mid_h, wo_h, w_h, teach_h,
    high_o, grad_o,
    q_v, kn_v, vn_v, ck_v, cv_v, ent_v, wo_v, wy, flm, fh, ft, sb, sr, tb, att, joint, es, ex, ec, grad_v,
    part1, part2, gath,
    ssem, rsem, lsem,
):
    g = lax.axis_index("group")
    t = lax.axis_index("tensor")
    y, zl, c = g // 4, (g // 2) % 2, g % 2
    zh, x = t // 4, t % 4

    def dev(dy=0, dzl=0, dc=0, dz=0, dx=0):
        yy = xor4(y, dy)
        return (yy * 4 + ((zl + dzl) % 2) * 2 + (c + dc) % 2, xor4(zh, dz) * 4 + xor4(x, dx))

    sent = []
    counts = [0, 0]

    def send(src, dst, peer):
        i = counts[0]
        counts[0] += 1
        copy = pltpu.make_async_remote_copy(
            src_ref=src, dst_ref=dst, send_sem=ssem.at[i], recv_sem=rsem.at[i],
            device_id=peer, device_id_type=MESH,
        )
        copy.start()
        sent.append(copy)
        return copy

    def load(src, dst):
        i = counts[1]
        counts[1] += 1
        copy = pltpu.make_async_copy(src, dst, lsem.at[i])
        copy.start()
        return copy

    barrier = pltpu.get_barrier_semaphore()
    peers = [dict(dx=1), dict(dx=3), dict(dz=1), dict(dz=3), dict(dy=1), dict(dy=2), dict(dy=3),
             dict(dzl=1), dict(dc=1), dict(dzl=1, dc=1)]
    for p in peers:
        pl.semaphore_signal(barrier, inc=1, device_id=dev(**p), device_id_type=MESH)

    l_att = [load(q_h, q_v), load(kn_h, kn_v), load(ck_h, ck_v), load(vn_h, vn_v), load(cv_h, cv_v)]
    l_w = load(w_h, wy.at[0])
    l_f = [load(low_h, flm.at[c, y, zl, 0]), load(mid_h, flm.at[c, y, zl, 1])]
    l_wo = []
    for i, (kx, kz) in enumerate((kx, kz) for kx in KX_ORDER for kz in KZ_ORDER):
        owner = xor4(zh, kz) * 4 + xor4(x, kx)
        l_wo.append(load(wo_h.at[:, pl.ds(pl.multiple_of(owner * 512, 512), 512)], wo_v.at[i]))
    l_ent = load(ent_h, ent_v)

    total = acc[0] + acc[1] + acc[2] + acc[3]
    scale = 4.0 / jnp.full((32, 128), total, jnp.int32).astype(F32)
    place = lax.broadcasted_iota(jnp.int32, (32, 128), 0)
    sb[...] = jnp.where(place < jnp.full((32, 128), acc[x], jnp.int32), scale, 0.0)

    pl.semaphore_wait(barrier, len(peers))

    b1, b0 = zh // 2, zh % 2
    tpeer = (y * 4 + ((zl + b1) % 2) * 2 + (c + b0) % 2, t)
    tsrc = []
    for ky in range(4):
        col = (xor4(y, ky) * 4 + ((zl + b1) % 2) * 2 + (c + b0) % 2) * 256
        tsrc.append(teach_h.at[pl.ds(pl.multiple_of(x * 32, 32), 32), pl.ds(pl.multiple_of(col, 256), 256)])
    base_r, base_l = counts[0], counts[1]
    counts[0] += 5
    counts[1] += 5

    def teacher_remote(i):
        src, dst = (tsrc[i], tb.at[i]) if i < 4 else (sb, sr)
        return pltpu.make_async_remote_copy(
            src_ref=src, dst_ref=dst, send_sem=ssem.at[base_r + i], recv_sem=rsem.at[base_r + i],
            device_id=tpeer, device_id_type=MESH,
        )

    def teacher_local(i):
        src, dst = (tsrc[i], tb.at[i]) if i < 4 else (sb, sr)
        return pltpu.make_async_copy(src, dst, lsem.at[base_l + i])

    @pl.when(zh != 0)
    def _():
        for i in range(5):
            teacher_remote(i).start()

    @pl.when(zh == 0)
    def _():
        for i in range(5):
            teacher_local(i).start()

    for cp in l_f:
        cp.wait()
    lm_zl = send(flm.at[c, y, zl], flm.at[c, y, zl], dev(dzl=1))
    lm_c = send(flm.at[c, y, zl], flm.at[c, y, zl], dev(dc=1))
    l_w.wait()
    w_y1 = send(wy.at[0], wy.at[1], dev(dy=1))
    w_y3 = send(wy.at[0], wy.at[3], dev(dy=3))

    for cp in l_att:
        cp.wait()
    inv = 128 ** (-0.5)
    for s in range(4):
        rows = slice(s * 32, s * 32 + 32)
        query = jnp.concatenate([q_v[rows, h * 128 : h * 128 + 128] for h in range(4)], axis=0)
        s_cache = dot_nt(query, ck_v[s]) * inv
        s_new = dot_nt(query, kn_v[...]) * inv
        slot = lax.broadcasted_iota(jnp.int32, (128, 512), 1)
        s_cache = jnp.where(slot < clen[s], s_cache, -jnp.inf)
        col = lax.broadcasted_iota(jnp.int32, (128, 128), 1) - s * 32
        row = lax.broadcasted_iota(jnp.int32, (128, 128), 0) % 32
        s_new = jnp.where((col >= 0) & (col <= row), s_new, -jnp.inf)
        top = jnp.maximum(jnp.max(s_cache, axis=1, keepdims=True), jnp.max(s_new, axis=1, keepdims=True))
        p_cache = jnp.exp(s_cache - top)
        p_new = jnp.exp(s_new - top)
        tot = jnp.sum(p_cache, axis=1, keepdims=True) + jnp.sum(p_new, axis=1, keepdims=True)
        mixed = dot(p_cache.astype(BF16), cv_v[s]) + dot(p_new.astype(BF16), vn_v[...])
        result = (mixed / tot).astype(BF16)
        for h in range(4):
            att[rows, h * 128 : h * 128 + 128] = result[h * 32 : h * 32 + 32]

    def begin(parts):
        return [Part(parts[i * 10 : i * 10 + 10], *PARTS[i]) for i in range(4)]

    def partner(p, first, k):
        return dev(dx=k) if p.x_first == first else dev(dz=k)

    def send_1(p, j):
        return send(p.s1.at[j], p.r1.at[j], partner(p, True, p.a))

    def step_2(parts, c1b):
        out = []
        for p, cp in zip(parts, c1b):
            cp.wait_recv()
            p.s2[...] = (p.k1[1] + p.r1[1].astype(F32)).astype(BF16)
            out.append(send(p.s2, p.r2, partner(p, True, p.b)))
        return out

    def step_3(parts, c1a, c2):
        for p, cp in zip(parts, c1a):
            cp.wait_recv()
            p.k1[0] = p.k1[0] + p.r1[0].astype(F32)
        out = []
        for p, cp in zip(parts, c2):
            cp.wait_recv()
            p.s3[...] = (p.k1[0, 2:4] + p.r2[2:4].astype(F32)).astype(BF16)
            out.append(send(p.s3, p.r3, partner(p, False, p.a2)))
        for p in parts:
            p.k2[...] = p.k1[0, 0:2] + p.r2[0:2].astype(F32)
        return out

    def step_4(parts, c3):
        out = []
        for p, cp in zip(parts, c3):
            cp.wait_recv()
            p.s4[...] = (p.k2[1] + p.r3[1].astype(F32)).astype(BF16)
            out.append(send(p.s4, p.r4, partner(p, False, p.b2)))
        return out

    def final(p, cp):
        cp.wait_recv()
        return p.k2[0] + p.r3[0].astype(F32) + p.r4[...].astype(F32)

    parts = begin(part1)
    c1a, c1b = [None] * 4, [None] * 4
    a_v = att[...]
    for i, (kx, kz) in enumerate((kx, kz) for kx in KX_ORDER for kz in KZ_ORDER):
        l_wo[i].wait()
        value = dot(a_v, wo_v[i])
        for p, (start, size) in zip(parts, ROW_PARTS):
            p.store(kz, kx, slice(None), value[start : start + size])
        if i == 3:
            c1b[0], c1b[1] = send_1(parts[0], 1), send_1(parts[1], 1)
        if i == 7:
            c1a[0] = send_1(parts[0], 0)
        if i == 11:
            c1a[1] = send_1(parts[1], 0)
        if i == 12:
            c1b[2], c1b[3] = send_1(parts[2], 1), send_1(parts[3], 1)
        if i == 13:
            c1a[2] = send_1(parts[2], 0)
        if i == 14:
            c1a[3] = send_1(parts[3], 0)

    lm_zl.wait_recv()
    lm_c2 = send(flm.at[c, y, (zl + 1) % 2], flm.at[c, y, (zl + 1) % 2], dev(dc=1))
    c2 = step_2(parts, c1b)
    w_y1.wait_recv()
    w_2a = send(wy.at[1, pl.ds(0, 768)], wy.at[2, pl.ds(0, 768)], dev(dy=3))
    w_y3.wait_recv()
    w_2b = send(wy.at[3, pl.ds(768, 768)], wy.at[2, pl.ds(768, 768)], dev(dy=1))
    lm_y1 = send(flm.at[c, y], flm.at[c, y], dev(dy=1))
    lm_y3 = send(flm.at[c, y], flm.at[c, y], dev(dy=3))
    c3 = step_3(parts, c1a, c2)
    c4 = step_4(parts, c3)
    lm_c.wait_recv()
    lm_c2.wait_recv()
    w_2a.wait_recv()
    w_2b.wait_recv()
    groups = []
    for kz in range(4):
        zz = xor4(zh, kz)
        groups.append(((c + zz % 2) % 2, (zl + zz // 2) % 2))

    def join_lm(s, carry):
        rows = jnp.concatenate(
            [jnp.concatenate([flm[cc, y, zz, f, s] for f in range(2)], axis=1) for cc, zz in groups], axis=0
        )
        for ky in range(4):
            joint[s, :, ky * 256 : ky * 256 + 256] = dot(rows, wy[ky, 0:1024])
        return carry

    lax.fori_loop(0, 4, join_lm, 0)
    l_ent.wait()
    for p, cp, (start, size) in zip(parts, c4, ROW_PARTS):
        value = final(p, cp)
        value = (ent_v[start : start + size].astype(F32) + value).astype(BF16)
        for r in range(0, size, 16):
            fh[c, y, zl, (start + r) // 32, (start + r) % 32 : (start + r) % 32 + 16] = value[r : r + 16]
    h_zl = send(fh.at[c, y, zl], fh.at[c, y, zl], dev(dzl=1))
    h_c = send(fh.at[c, y, zl], fh.at[c, y, zl], dev(dc=1))
    o_high = load(fh.at[c, y, zl], high_o)
    h_zl.wait_recv()
    h_c2 = send(fh.at[c, y, (zl + 1) % 2], fh.at[c, y, (zl + 1) % 2], dev(dc=1))
    h_y1 = send(fh.at[c, y], fh.at[c, y], dev(dy=1))
    h_y3 = send(fh.at[c, y], fh.at[c, y], dev(dy=3))
    h_c.wait_recv()
    h_c2.wait_recv()

    parts = begin(part2)
    c1a, c1b = [None] * 4, [None] * 4
    for kx in KX_ORDER:
        s = xor4(x, kx)
        rows = jnp.concatenate([fh[cc, y, zz, s] for cc, zz in groups], axis=0)
        for ky in range(4):
            value = joint[s, :, ky * 256 : ky * 256 + 256] + dot(rows, wy[ky, 1024:1536])
            for half in range(2):
                at = ky * 256 + half * 128
                for p, (start, size) in zip(parts, COL_PARTS):
                    if start <= at < start + size:
                        for kz in range(4):
                            p.store(kz, kx, slice(at - start, at - start + 128),
                                    value[kz * 32 : kz * 32 + 32, half * 128 : half * 128 + 128])
        if kx == 2:
            c1b[0], c1b[1] = send_1(parts[0], 1), send_1(parts[1], 1)
        if kx == 1:
            c1a[0] = send_1(parts[0], 0)
        if kx == 3:
            c1a[1] = send_1(parts[1], 0)
    for i in (2, 3):
        c1b[i] = send_1(parts[i], 1)
    for i in (2, 3):
        c1a[i] = send_1(parts[i], 0)

    y1, y3, y2 = xor4(y, 1), xor4(y, 3), xor4(y, 2)
    lm_y1.wait_recv()
    lm_2a = send(flm.at[c, y1, 0], flm.at[c, y1, 0], dev(dy=3))
    lm_y3.wait_recv()
    lm_2b = send(flm.at[c, y3, 1], flm.at[c, y3, 1], dev(dy=1))
    lm_f = [send(flm.at[c, y1], flm.at[c, y1], dev(dc=1)), send(flm.at[c, y3], flm.at[c, y3], dev(dc=1))]
    c2 = step_2(parts, c1b)
    lm_2a.wait_recv()
    lm_2b.wait_recv()
    lm_f.append(send(flm.at[c, y2], flm.at[c, y2], dev(dc=1)))
    h_y1.wait_recv()
    h_2a = send(fh.at[c, y1, 0], fh.at[c, y1, 0], dev(dy=3))
    h_y3.wait_recv()
    h_2b = send(fh.at[c, y3, 1], fh.at[c, y3, 1], dev(dy=1))
    h_f = [send(fh.at[c, y1], fh.at[c, y1], dev(dc=1)), send(fh.at[c, y3], fh.at[c, y3], dev(dc=1))]
    c3 = step_3(parts, c1a, c2)
    for cp in lm_f:
        cp.wait_recv()

    def turn(lo, hi, feature):
        def body(j, carry):
            kx, kz = j // 4, j % 4
            zz = xor4(zh, kz)
            cc, ll = (c + zz % 2) % 2, (zl + zz // 2) % 2
            s = xor4(x, kx)
            if feature < 2:
                blocks = [flm[cc, xor4(y, ky), ll, feature, s] for ky in range(4)]
            else:
                blocks = [fh[cc, xor4(y, ky), ll, s] for ky in range(4)]
            rows = jnp.concatenate(blocks, axis=0)
            ft[feature, :, pl.ds(pl.multiple_of(j * 128, 128), 128)] = rows.T
            return carry

        lax.fori_loop(lo, hi, body, 0)

    turn(0, 6, 0)
    c4 = step_4(parts, c3)
    turn(6, 12, 0)
    h_2a.wait_recv()
    h_2b.wait_recv()
    h_f.append(send(fh.at[c, y2], fh.at[c, y2], dev(dc=1)))

    @pl.when(zh != 0)
    def _():
        for i in range(5):
            teacher_remote(i).wait()

    @pl.when(zh == 0)
    def _():
        for i in range(5):
            teacher_local(i).wait()

    row_scale = sr[...]
    for p, cp, (start, size) in zip(parts, c4, COL_PARTS):
        value = final(p, cp)
        for off in range(0, size, 128):
            at = start + off
            ky, lanes = at // 256, slice(at % 256, at % 256 + 128)
            err = (value[:, off : off + 128] - tb[ky, :, lanes].astype(F32)) * row_scale
            es[ky, :, lanes] = err.astype(BF16)
    e_y = [send(es.at[ky], ex.at[ky], dev(dy=ky)) for ky in (1, 3, 2)]
    ex[0] = es[0]
    turn(12, 16, 0)
    for cp in e_y:
        cp.wait_recv()
    for p, (start, size), gb in zip(parts, ROW_PARTS, gath):
        for r in range(0, size, 16):
            gb[0, 0, r : r + 16] = ex[(start + r) // 32, (start + r) % 32 : (start + r) % 32 + 16]
    cps = [send(gb.at[0, 0], gb.at[0, 1], partner(p, False, p.a2)) for p, gb in zip(parts, gath)]
    turn(0, 4, 1)
    for cp in cps:
        cp.wait_recv()
    cps = [send(gb.at[0, pl.ds(0, 2)], gb.at[0, pl.ds(2, 2)], partner(p, False, p.b2)) for p, gb in zip(parts, gath)]
    turn(4, 10, 1)
    for cp in cps:
        cp.wait_recv()
    cps = [send(gb.at[0], gb.at[1], partner(p, True, p.a)) for p, gb in zip(parts, gath)]
    turn(10, 16, 1)
    for cp in cps:
        cp.wait_recv()
    cps = [send(gb.at[pl.ds(0, 2)], gb.at[pl.ds(2, 2)], partner(p, True, p.b)) for p, gb in zip(parts, gath)]
    for cp in h_f:
        cp.wait_recv()
    turn(0, 16, 2)
    for cp in cps:
        cp.wait_recv()

    def slot(p, gb, kz, kx):
        first, second = (kx, kz) if p.x_first else (kz, kx)
        return gb[(0, p.a, p.b, 2).index(first), (0, p.a2, p.b2, 2).index(second)]

    for kx in range(4):
        for kz in range(4):
            j = kx * 4 + kz
            ec[j * 128 : j * 128 + 128] = jnp.concatenate(
                [slot(p, gb, kz, kx) for p, gb in zip(parts, gath)], axis=0
            )
    outs = []
    for f in range(3):
        grad_v[f] = dot(ft[f], ec[...])
        outs.append(load(grad_v.at[f], grad_o.at[f]))
    for cp in outs:
        cp.wait()
    o_high.wait()
    for cp in sent:
        cp.wait_send()


def shards(
    queries, keys_new, values_new, cache_keys, cache_values, cache_len, accepted,
    entering, low_feature, mid_feature, out_proj, join_weight, teacher,
):
    anywhere = pl.BlockSpec(memory_space=pl.ANY)
    scalars = pl.BlockSpec(memory_space=pltpu.SMEM)
    scratch = [
        pltpu.VMEM((128, 512), BF16),
        pltpu.VMEM((128, 128), BF16),
        pltpu.VMEM((128, 128), BF16),
        pltpu.VMEM((4, 512, 128), BF16),
        pltpu.VMEM((4, 512, 128), BF16),
        pltpu.VMEM((128, 512), BF16),
        pltpu.VMEM((16, 512, 512), BF16),
        pltpu.VMEM((4, 1536, 256), BF16),
        pltpu.VMEM((2, 4, 2, 2, 4, 32, 512), BF16),
        pltpu.VMEM((2, 4, 2, 4, 32, 512), BF16),
        pltpu.VMEM((3, 512, 2048), BF16),
        pltpu.VMEM((32, 128), F32),
        pltpu.VMEM((32, 128), F32),
        pltpu.VMEM((4, 32, 256), BF16),
        pltpu.VMEM((128, 512), BF16),
        pltpu.VMEM((4, 128, 1024), F32),
        pltpu.VMEM((4, 32, 256), BF16),
        pltpu.VMEM((4, 32, 256), BF16),
        pltpu.VMEM((2048, 256), BF16),
        pltpu.VMEM((3, 512, 256), F32),
        [s for _, size in ROW_PARTS for s in part_shapes(size, 512)],
        [s for _, size in COL_PARTS for s in part_shapes(32, size)],
        [pltpu.VMEM((4, 4, size, 256), BF16) for _, size in ROW_PARTS],
        pltpu.SemaphoreType.DMA((COPIES,)),
        pltpu.SemaphoreType.DMA((COPIES,)),
        pltpu.SemaphoreType.DMA((LOADS,)),
    ]
    high, grad = pl.pallas_call(
        kernel,
        out_shape=(
            jax.ShapeDtypeStruct((4, 32, 512), BF16),
            jax.ShapeDtypeStruct((3, 512, 256), F32),
        ),
        in_specs=[anywhere] * 5 + [scalars] * 2 + [anywhere] * 6,
        out_specs=(anywhere, anywhere),
        scratch_shapes=scratch,
        compiler_params=pltpu.CompilerParams(
            collective_id=0, has_side_effects=True, vmem_limit_bytes=60 * 2**20
        ),
        name="verify_join",
    )(
        queries, keys_new, values_new, cache_keys.reshape(4, 512, 128), cache_values.reshape(4, 512, 128),
        cache_len, accepted, entering, low_feature.reshape(4, 32, 512), mid_feature.reshape(4, 32, 512),
        out_proj, join_weight.reshape(1536, 256), teacher,
    )
    return high.reshape(128, 512), grad


def solution(mesh):
    return jax.shard_map(
        shards,
        mesh=mesh,
        in_specs=(
            P("group", "tensor"),
            P("group", "tensor"),
            P("group", "tensor"),
            P("group", "tensor", None, None),
            P("group", "tensor", None, None),
            P("group"),
            P("group"),
            P("group", "tensor"),
            P("group", "tensor"),
            P("group", "tensor"),
            P("tensor", None),
            P(None, "tensor", "group"),
            P("group", None),
        ),
        out_specs=(P("group", "tensor"), P(None, "tensor", "group")),
        check_vma=False,
    )
```

time: 408 us -> 101 us (0.25)
  waiting for transfers between devices: 342 us -> 0 us
  Pallas kernels: 0 us -> 96.2 us
  matrix products: 23.2 us -> 0 us
  between operations: 16.3 us -> 0.64 us
  starting transfers between devices: 6.96 us -> 0 us
  local copies, waits for them, and re-layouts: 11 us -> 4.22 us
  other arithmetic: 5.55 us -> 0 us
    psum x1 -> x0, waiting for transfers between devices: 190 us -> none  [shards(): joined = lax.psum(joined_part, 'tensor')]
    reduce_scatter x1 -> x0, waiting for transfers between devices: 145 us -> none  [shards(): lax.psum_scatter(partial_value, 'tensor', scatter_dimension=1, tiled=True)]
    pallas_call x0 -> x1, Pallas kernels: none -> 96.2 us  [shards(): pl.pallas_call(kernel, out_shape=(jax.ShapeDtypeStruct((4, 32, 512), BF16...]
    dot_general x7 -> x0, matrix products: 23.2 us -> none  [the longest x1 7.79 us: shards(): jnp.dot(features, lax.all_gather(local_weight, 'group', axis=1, tiled=Tru...]
    dot_general x1 -> x0, local copies, waits for them, and re-layouts: 8.67 us -> none  [shards(): lax.dot_general(gathered, error_cols, (((0,), (0,)), ((), ())), preferred...]
    all_to_all x1 -> x0, starting transfers between devices: 6.79 us -> none  [shards(): lax.all_to_all(error, 'group', split_axis=1, concat_axis=0, tiled=True)]
    all_to_all x1 -> x0, waiting for transfers between devices: 6.65 us -> none  [shards(): lax.all_to_all(error, 'group', split_axis=1, concat_axis=0, tiled=True)]
    unnamed x16 -> x2, local copies, waits for them, and re-layouts: 0.04 us -> 4.22 us
  transfers between devices with their start and end apart: 5 -> 0, of which waited for: 3 -> 0; matrix products, arithmetic and copies ran while one was open for 4% -> 0% of each run, Pallas kernels for 0% -> 0%
where the time goes in v1:
time: 101 us
  Pallas kernels  96.2 us (95%)
  local copies, waits for them, and re-layouts  4.22 us (4%)
    pallas_call x1, Pallas kernels, shards(): pl.pallas_call(kernel, out_shape=(jax.ShapeDtypeStruct((4, 32, 512), BF16...  96.2 us
    unnamed x2, local copies, waits for them, and re-layouts  4.22 us

profile of v1, /device:TPU:32, one launch (start us, length us, event | category | flops | bytes accessed | tf_op | source)
XLA Modules:
  0.0 101.1 jit_solution(16404732155589895391)
XLA Ops:
  0.6 96.2 %verify_join.1 = (bf16[4,32,512]{2,1,0:T(8,128)(2,1)}, f32[3,512,256]{2,1,0:T(8,128)}) custom-call(bf16[128,512]{1,0:T(8,128)(2,1)} %q_h.1, bf16[128,128]{1,0:T(8,128)(2,1)} %kn_h.1, bf16[128,128]{1,0:T(8,128)(2,1)} %vn_h.1, bf16[4,512,128]{2,1,0:T(8,128)(2,1)} %bitcast.7, bf16[4,512,128]{2,1,0:T(8,128)(2,1)} %bitcast.8, s32[4]{0:T(128)} %clen.1, s32[4]{0:T(128)} %acc.1, ...), custom_call_target="tpu_custom_call" | custom-call | tf_op jit(solution)/shard_map/verify_join/pallas_call | solution.py:464
  96.9 1.6 %copy.17 = bf16[128,512]{1,0:T(8,128)(2,1)} copy(bf16[128,512]{1,0:T(8,128)(2,1)} %bitcast.11) | data formatting | bytes 262144
  98.4 2.7 %copy.18 = f32[3,512,256]{2,1,0:T(8,128)} copy(f32[3,512,256]{2,1,0:T(8,128)} %get-tuple-element.9) | data formatting | bytes 3145728

commit v2 on v1

--- a/solution.py
+++ b/solution.py
@@ -61,7 +61,6 @@
 
 PARTS = ((True, 1, 1), (True, 3, 3), (False, 1, 1), (False, 3, 3))
 ROW_PARTS = ((0, 48), (48, 48), (96, 16), (112, 16))
-COL_PARTS = ((0, 384), (384, 384), (768, 128), (896, 128))
 KX_ORDER = (2, 1, 3, 0)
 KZ_ORDER = (2, 1, 3, 0)
 
@@ -69,8 +68,8 @@
 def kernel(
     q_h, kn_h, vn_h, ck_h, cv_h, clen, acc, ent_h, low_h, mid_h, wo_h, w_h, teach_h,
     high_o, grad_o,
-    q_v, kn_v, vn_v, ck_v, cv_v, ent_v, wo_v, wy, flm, fh, ft, sb, sr, tb, att, joint, es, ex, ec, grad_v,
-    part1, part2, gath,
+    q_v, kn_v, vn_v, ck_v, cv_v, ent_v, wo_v, wy, flm, fh, ft, sb, sr, tb, att, joint, xs, xr, zk, zs, zr, es, gath,
+    grad_v, part1,
     ssem, rsem, lsem,
 ):
     g = lax.axis_index("group")
@@ -104,7 +103,7 @@
         return copy
 
     barrier = pltpu.get_barrier_semaphore()
-    peers = [dict(dx=1), dict(dx=3), dict(dz=1), dict(dz=3), dict(dy=1), dict(dy=2), dict(dy=3),
+    peers = [dict(dx=1), dict(dx=2), dict(dx=3), dict(dz=1), dict(dz=2), dict(dz=3), dict(dy=1), dict(dy=2), dict(dy=3),
              dict(dzl=1), dict(dc=1), dict(dzl=1, dc=1)]
     for p in peers:
         pl.semaphore_signal(barrier, inc=1, device_id=dev(**p), device_id_type=MESH)
@@ -123,51 +122,9 @@
     place = lax.broadcasted_iota(jnp.int32, (32, 128), 0)
     sb[...] = jnp.where(place < jnp.full((32, 128), acc[x], jnp.int32), scale, 0.0)
 
-    pl.semaphore_wait(barrier, len(peers))
-
-    b1, b0 = zh // 2, zh % 2
-    tpeer = (y * 4 + ((zl + b1) % 2) * 2 + (c + b0) % 2, t)
-    tsrc = []
-    for ky in range(4):
-        col = (xor4(y, ky) * 4 + ((zl + b1) % 2) * 2 + (c + b0) % 2) * 256
-        tsrc.append(teach_h.at[pl.ds(pl.multiple_of(x * 32, 32), 32), pl.ds(pl.multiple_of(col, 256), 256)])
-    base_r, base_l = counts[0], counts[1]
-    counts[0] += 5
-    counts[1] += 5
-
-    def teacher_remote(i):
-        src, dst = (tsrc[i], tb.at[i]) if i < 4 else (sb, sr)
-        return pltpu.make_async_remote_copy(
-            src_ref=src, dst_ref=dst, send_sem=ssem.at[base_r + i], recv_sem=rsem.at[base_r + i],
-            device_id=tpeer, device_id_type=MESH,
-        )
-
-    def teacher_local(i):
-        src, dst = (tsrc[i], tb.at[i]) if i < 4 else (sb, sr)
-        return pltpu.make_async_copy(src, dst, lsem.at[base_l + i])
-
-    @pl.when(zh != 0)
-    def _():
-        for i in range(5):
-            teacher_remote(i).start()
-
-    @pl.when(zh == 0)
-    def _():
-        for i in range(5):
-            teacher_local(i).start()
-
-    for cp in l_f:
-        cp.wait()
-    lm_zl = send(flm.at[c, y, zl], flm.at[c, y, zl], dev(dzl=1))
-    lm_c = send(flm.at[c, y, zl], flm.at[c, y, zl], dev(dc=1))
-    l_w.wait()
-    w_y1 = send(wy.at[0], wy.at[1], dev(dy=1))
-    w_y3 = send(wy.at[0], wy.at[3], dev(dy=3))
-
-    for cp in l_att:
-        cp.wait()
     inv = 128 ** (-0.5)
-    for s in range(4):
+
+    def attend(s):
         rows = slice(s * 32, s * 32 + 32)
         query = jnp.concatenate([q_v[rows, h * 128 : h * 128 + 128] for h in range(4)], axis=0)
         s_cache = dot_nt(query, ck_v[s]) * inv
@@ -185,6 +142,52 @@
         result = (mixed / tot).astype(BF16)
         for h in range(4):
             att[rows, h * 128 : h * 128 + 128] = result[h * 32 : h * 32 + 32]
+
+    for cp in l_att:
+        cp.wait()
+    attend(0)
+    pl.semaphore_wait(barrier, len(peers))
+    w_y1 = send(w_h, wy.at[1], dev(dy=1))
+    w_y3 = send(w_h, wy.at[3], dev(dy=3))
+
+    b1, b0 = zh // 2, zh % 2
+    tpeer = (y * 4 + ((zl + b1) % 2) * 2 + (c + b0) % 2, t)
+    tsrc = []
+    for ky in range(4):
+        col = (xor4(y, ky) * 4 + ((zl + b1) % 2) * 2 + (c + b0) % 2) * 256
+        tsrc.append(teach_h.at[pl.ds(pl.multiple_of(x * 32, 32), 32), pl.ds(pl.multiple_of(col, 256), 256)])
+    base_r, base_l = counts[0], counts[1]
+    counts[0] += 5
+    counts[1] += 5
+
+    def teacher_remote(i):
+        src, dst = (tsrc[i], tb.at[i]) if i < 4 else (sb, sr)
+        return pltpu.make_async_remote_copy(
+            src_ref=src, dst_ref=dst, send_sem=ssem.at[base_r + i], recv_sem=rsem.at[base_r + i],
+            device_id=tpeer, device_id_type=MESH,
+        )
+
+    def teacher_local(i):
+        src, dst = (tsrc[i], tb.at[i]) if i < 4 else (sb, sr)
+        return pltpu.make_async_copy(src, dst, lsem.at[base_l + i])
+
+    @pl.when(zh != 0)
+    def _():
+        for i in range(5):
+            teacher_remote(i).start()
+
+    @pl.when(zh == 0)
+    def _():
+        for i in range(5):
+            teacher_local(i).start()
+
+    for cp in l_f:
+        cp.wait()
+    lm_zl = send(flm.at[c, y, zl], flm.at[c, y, zl], dev(dzl=1))
+    lm_c = send(flm.at[c, y, zl], flm.at[c, y, zl], dev(dc=1))
+
+    for s in range(1, 4):
+        attend(s)
 
     def begin(parts):
         return [Part(parts[i * 10 : i * 10 + 10], *PARTS[i]) for i in range(4)]
@@ -256,28 +259,20 @@
     w_2a = send(wy.at[1, pl.ds(0, 768)], wy.at[2, pl.ds(0, 768)], dev(dy=3))
     w_y3.wait_recv()
     w_2b = send(wy.at[3, pl.ds(768, 768)], wy.at[2, pl.ds(768, 768)], dev(dy=1))
-    lm_y1 = send(flm.at[c, y], flm.at[c, y], dev(dy=1))
-    lm_y3 = send(flm.at[c, y], flm.at[c, y], dev(dy=3))
     c3 = step_3(parts, c1a, c2)
     c4 = step_4(parts, c3)
     lm_c.wait_recv()
     lm_c2.wait_recv()
+    l_w.wait()
     w_2a.wait_recv()
     w_2b.wait_recv()
-    groups = []
-    for kz in range(4):
-        zz = xor4(zh, kz)
-        groups.append(((c + zz % 2) % 2, (zl + zz // 2) % 2))
-
-    def join_lm(s, carry):
-        rows = jnp.concatenate(
-            [jnp.concatenate([flm[cc, y, zz, f, s] for f in range(2)], axis=1) for cc, zz in groups], axis=0
-        )
+    lm_y1 = send(flm.at[c, y], flm.at[c, y], dev(dy=1))
+    lm_y3 = send(flm.at[c, y], flm.at[c, y], dev(dy=3))
+    groups = [((c + j % 2) % 2, (zl + j // 2) % 2) for j in range(4)]
+    for j, (cc, ll) in enumerate(groups):
+        rows = jnp.concatenate([flm[cc, y, ll, f].reshape(128, 512) for f in range(2)], axis=1)
         for ky in range(4):
-            joint[s, :, ky * 256 : ky * 256 + 256] = dot(rows, wy[ky, 0:1024])
-        return carry
-
-    lax.fori_loop(0, 4, join_lm, 0)
+            joint[j, :, :, ky * 256 : ky * 256 + 256] = dot(rows, wy[ky, 0:1024]).reshape(4, 32, 256)
     l_ent.wait()
     for p, cp, (start, size) in zip(parts, c4, ROW_PARTS):
         value = final(p, cp)
@@ -287,37 +282,56 @@
     h_zl = send(fh.at[c, y, zl], fh.at[c, y, zl], dev(dzl=1))
     h_c = send(fh.at[c, y, zl], fh.at[c, y, zl], dev(dc=1))
     o_high = load(fh.at[c, y, zl], high_o)
+
+    to_x = [None] * 4
+
+    def join(j):
+        cc, ll = groups[j]
+        rows = fh[cc, y, ll].reshape(128, 512)
+        for ky in range(4):
+            cols = slice(ky * 256, ky * 256 + 256)
+            value = joint[j, :, :, cols] + dot(rows, wy[ky, 1024:1536]).reshape(4, 32, 256)
+            joint[j, :, :, cols] = value
+            xs[j, :, :, cols] = value.astype(BF16)
+        to_x[j] = [send(xs.at[j, xor4(x, k)], xr.at[j, k], dev(dx=k)) for k in (2, 1, 3)]
+
+    base_z = counts[0]
+    counts[0] += 8
+
+    def to_z(j):
+        k = xor4(zh, j)
+        return pltpu.make_async_remote_copy(
+            src_ref=zs.at[j], dst_ref=zr.at[k], send_sem=ssem.at[base_z + j], recv_sem=rsem.at[base_z + 4 + k],
+            device_id=(g, j * 4 + x), device_id_type=MESH,
+        )
+
+    def sum_x(j):
+        value = joint[j, x]
+        for cp, k in zip(to_x[j], (2, 1, 3)):
+            cp.wait_recv()
+        for k in (1, 2, 3):
+            value = value + xr[j, k].astype(F32)
+        zk[j] = value
+        zs[j] = value.astype(BF16)
+
+        @pl.when(zh != j)
+        def _():
+            to_z(j).start()
+
+    join(0)
+    h_c.wait_recv()
+    join(1)
     h_zl.wait_recv()
     h_c2 = send(fh.at[c, y, (zl + 1) % 2], fh.at[c, y, (zl + 1) % 2], dev(dc=1))
+    join(2)
+    sum_x(0)
+    h_c2.wait_recv()
+    join(3)
     h_y1 = send(fh.at[c, y], fh.at[c, y], dev(dy=1))
     h_y3 = send(fh.at[c, y], fh.at[c, y], dev(dy=3))
-    h_c.wait_recv()
-    h_c2.wait_recv()
-
-    parts = begin(part2)
-    c1a, c1b = [None] * 4, [None] * 4
-    for kx in KX_ORDER:
-        s = xor4(x, kx)
-        rows = jnp.concatenate([fh[cc, y, zz, s] for cc, zz in groups], axis=0)
-        for ky in range(4):
-            value = joint[s, :, ky * 256 : ky * 256 + 256] + dot(rows, wy[ky, 1024:1536])
-            for half in range(2):
-                at = ky * 256 + half * 128
-                for p, (start, size) in zip(parts, COL_PARTS):
-                    if start <= at < start + size:
-                        for kz in range(4):
-                            p.store(kz, kx, slice(at - start, at - start + 128),
-                                    value[kz * 32 : kz * 32 + 32, half * 128 : half * 128 + 128])
-        if kx == 2:
-            c1b[0], c1b[1] = send_1(parts[0], 1), send_1(parts[1], 1)
-        if kx == 1:
-            c1a[0] = send_1(parts[0], 0)
-        if kx == 3:
-            c1a[1] = send_1(parts[1], 0)
-    for i in (2, 3):
-        c1b[i] = send_1(parts[i], 1)
-    for i in (2, 3):
-        c1a[i] = send_1(parts[i], 0)
+    sum_x(1)
+    sum_x(2)
+    sum_x(3)
 
     y1, y3, y2 = xor4(y, 1), xor4(y, 3), xor4(y, 2)
     lm_y1.wait_recv()
@@ -325,22 +339,10 @@
     lm_y3.wait_recv()
     lm_2b = send(flm.at[c, y3, 1], flm.at[c, y3, 1], dev(dy=1))
     lm_f = [send(flm.at[c, y1], flm.at[c, y1], dev(dc=1)), send(flm.at[c, y3], flm.at[c, y3], dev(dc=1))]
-    c2 = step_2(parts, c1b)
-    lm_2a.wait_recv()
-    lm_2b.wait_recv()
-    lm_f.append(send(flm.at[c, y2], flm.at[c, y2], dev(dc=1)))
-    h_y1.wait_recv()
-    h_2a = send(fh.at[c, y1, 0], fh.at[c, y1, 0], dev(dy=3))
-    h_y3.wait_recv()
-    h_2b = send(fh.at[c, y3, 1], fh.at[c, y3, 1], dev(dy=1))
-    h_f = [send(fh.at[c, y1], fh.at[c, y1], dev(dc=1)), send(fh.at[c, y3], fh.at[c, y3], dev(dc=1))]
-    c3 = step_3(parts, c1a, c2)
-    for cp in lm_f:
-        cp.wait_recv()
 
     def turn(lo, hi, feature):
         def body(j, carry):
-            kx, kz = j // 4, j % 4
+            kz, kx = j // 4, j % 4
             zz = xor4(zh, kz)
             cc, ll = (c + zz % 2) % 2, (zl + zz // 2) % 2
             s = xor4(x, kx)
@@ -354,13 +356,6 @@
 
         lax.fori_loop(lo, hi, body, 0)
 
-    turn(0, 6, 0)
-    c4 = step_4(parts, c3)
-    turn(6, 12, 0)
-    h_2a.wait_recv()
-    h_2b.wait_recv()
-    h_f.append(send(fh.at[c, y2], fh.at[c, y2], dev(dc=1)))
-
     @pl.when(zh != 0)
     def _():
         for i in range(5):
@@ -371,60 +366,90 @@
         for i in range(5):
             teacher_local(i).wait()
 
-    row_scale = sr[...]
-    for p, cp, (start, size) in zip(parts, c4, COL_PARTS):
-        value = final(p, cp)
-        for off in range(0, size, 128):
-            at = start + off
-            ky, lanes = at // 256, slice(at % 256, at % 256 + 128)
-            err = (value[:, off : off + 128] - tb[ky, :, lanes].astype(F32)) * row_scale
-            es[ky, :, lanes] = err.astype(BF16)
-    e_y = [send(es.at[ky], ex.at[ky], dev(dy=ky)) for ky in (1, 3, 2)]
-    ex[0] = es[0]
-    turn(12, 16, 0)
+    value = zk[zh]
+    for k in (1, 3, 2):
+        pltpu.make_async_remote_copy(
+            src_ref=zs.at[0], dst_ref=zr.at[k], send_sem=ssem.at[base_z], recv_sem=rsem.at[base_z + 4 + k],
+            device_id=dev(dz=k), device_id_type=MESH,
+        ).wait_recv()
+        value = value + zr[k].astype(F32)
+    row_scale = jnp.concatenate([sr[...], sr[...]], axis=1)
+    for ky in (1, 3, 2, 0):
+        err = (value[:, ky * 256 : ky * 256 + 256] - tb[ky].astype(F32)) * row_scale
+        if ky:
+            es[ky] = err.astype(BF16)
+        else:
+            gath[0, 0, 0] = err.astype(BF16)
+    e_y = [send(es.at[ky], gath.at[0, 0, ky], dev(dy=ky)) for ky in (1, 3, 2)]
+    e_z0 = {k: send(gath.at[0, 0, 0], gath.at[k, 0, 0], dev(dz=k)) for k in (2, 1, 3)}
     for cp in e_y:
         cp.wait_recv()
-    for p, (start, size), gb in zip(parts, ROW_PARTS, gath):
-        for r in range(0, size, 16):
-            gb[0, 0, r : r + 16] = ex[(start + r) // 32, (start + r) % 32 : (start + r) % 32 + 16]
-    cps = [send(gb.at[0, 0], gb.at[0, 1], partner(p, False, p.a2)) for p, gb in zip(parts, gath)]
-    turn(0, 4, 1)
-    for cp in cps:
+    rest = pl.ds(1, 3)
+    e_z1 = {k: send(gath.at[0, 0, rest], gath.at[k, 0, rest], dev(dz=k)) for k in (2, 1, 3)}
+    e_x = {0: [send(gath.at[0, 0], gath.at[0, k], dev(dx=k)) for k in (2, 1, 3)]}
+    h_y1.wait_recv()
+    h_2a = send(fh.at[c, y1, 0], fh.at[c, y1, 0], dev(dy=3))
+    h_y3.wait_recv()
+    h_2b = send(fh.at[c, y3, 1], fh.at[c, y3, 1], dev(dy=1))
+    h_f = [send(fh.at[c, y1], fh.at[c, y1], dev(dc=1)), send(fh.at[c, y3], fh.at[c, y3], dev(dc=1))]
+    lm_2a.wait_recv()
+    lm_2b.wait_recv()
+    lm_f.append(send(flm.at[c, y2], flm.at[c, y2], dev(dc=1)))
+    for k in (1, 3):
+        e_z0[k].wait_recv()
+        e_z1[k].wait_recv()
+        e_x[k] = [send(gath.at[k, 0], gath.at[k, q], dev(dx=q)) for q in (2, 1, 3)]
+    e_z0[2].wait_recv()
+    e_z1[2].wait_recv()
+    e_x[2] = [send(gath.at[2, 0], gath.at[2, q], dev(dx=q)) for q in (2, 1, 3)]
+    h_2a.wait_recv()
+    h_2b.wait_recv()
+    h_f.append(send(fh.at[c, y2], fh.at[c, y2], dev(dc=1)))
+    for cp in lm_f:
         cp.wait_recv()
-    cps = [send(gb.at[0, pl.ds(0, 2)], gb.at[0, pl.ds(2, 2)], partner(p, False, p.b2)) for p, gb in zip(parts, gath)]
-    turn(4, 10, 1)
-    for cp in cps:
-        cp.wait_recv()
-    cps = [send(gb.at[0], gb.at[1], partner(p, True, p.a)) for p, gb in zip(parts, gath)]
-    turn(10, 16, 1)
-    for cp in cps:
-        cp.wait_recv()
-    cps = [send(gb.at[pl.ds(0, 2)], gb.at[pl.ds(2, 2)], partner(p, True, p.b)) for p, gb in zip(parts, gath)]
+    turn(0, 16, 0)
+    turn(0, 16, 1)
     for cp in h_f:
         cp.wait_recv()
     turn(0, 16, 2)
-    for cp in cps:
-        cp.wait_recv()
-
-    def slot(p, gb, kz, kx):
-        first, second = (kx, kz) if p.x_first else (kz, kx)
-        return gb[(0, p.a, p.b, 2).index(first), (0, p.a2, p.b2, 2).index(second)]
-
-    for kx in range(4):
-        for kz in range(4):
-            j = kx * 4 + kz
-            ec[j * 128 : j * 128 + 128] = jnp.concatenate(
-                [slot(p, gb, kz, kx) for p, gb in zip(parts, gath)], axis=0
-            )
+
     outs = []
-    for f in range(3):
-        grad_v[f] = dot(ft[f], ec[...])
-        outs.append(load(grad_v.at[f], grad_o.at[f]))
+    for k in (0, 1, 3, 2):
+        for cp in e_x[k]:
+            cp.wait_recv()
+        block = gath[k].reshape(512, 256)
+        for f in range(3):
+            value = dot(ft[f, :, k * 512 : k * 512 + 512], block)
+            if k:
+                value = grad_v[f] + value
+            grad_v[f] = value
+            if k == 2:
+                outs.append(load(grad_v.at[f], grad_o.at[f]))
     for cp in outs:
         cp.wait()
     o_high.wait()
     for cp in sent:
         cp.wait_send()
+    for j in range(4):
+
+        @pl.when(zh != j)
+        def _():
+            to_z(j).wait_send()
+
+
+def deliver(high_i, grad_i, high_o, grad_o, high_v, grad_v, sem):
+    ins = [pltpu.make_async_copy(high_i, high_v, sem.at[0, 0])]
+    outs = [pltpu.make_async_copy(high_v, high_o, sem.at[1, 0])]
+    for f in range(3):
+        ins.append(pltpu.make_async_copy(grad_i.at[f], grad_v.at[f], sem.at[0, f + 1]))
+        outs.append(pltpu.make_async_copy(grad_v.at[f], grad_o.at[f], sem.at[1, f + 1]))
+    for copy in ins:
+        copy.start()
+    for before, after in zip(ins, outs):
+        before.wait()
+        after.start()
+    for copy in outs:
+        copy.wait()
 
 
 def shards(
@@ -432,6 +457,7 @@
     entering, low_feature, mid_feature, out_proj, join_weight, teacher,
 ):
     anywhere = pl.BlockSpec(memory_space=pl.ANY)
+    far = pl.BlockSpec(memory_space=pltpu.HBM)
     scalars = pl.BlockSpec(memory_space=pltpu.SMEM)
     scratch = [
         pltpu.VMEM((128, 512), BF16),
@@ -449,14 +475,16 @@
         pltpu.VMEM((32, 128), F32),
         pltpu.VMEM((4, 32, 256), BF16),
         pltpu.VMEM((128, 512), BF16),
-        pltpu.VMEM((4, 128, 1024), F32),
+        pltpu.VMEM((4, 4, 32, 1024), F32),
+        pltpu.VMEM((4, 4, 32, 1024), BF16),
+        pltpu.VMEM((4, 4, 32, 1024), BF16),
+        pltpu.VMEM((4, 32, 1024), F32),
+        pltpu.VMEM((4, 32, 1024), BF16),
+        pltpu.VMEM((4, 32, 1024), BF16),
         pltpu.VMEM((4, 32, 256), BF16),
-        pltpu.VMEM((4, 32, 256), BF16),
-        pltpu.VMEM((2048, 256), BF16),
+        pltpu.VMEM((4, 4, 4, 32, 256), BF16),
         pltpu.VMEM((3, 512, 256), F32),
         [s for _, size in ROW_PARTS for s in part_shapes(size, 512)],
-        [s for _, size in COL_PARTS for s in part_shapes(32, size)],
-        [pltpu.VMEM((4, 4, size, 256), BF16) for _, size in ROW_PARTS],
         pltpu.SemaphoreType.DMA((COPIES,)),
         pltpu.SemaphoreType.DMA((COPIES,)),
         pltpu.SemaphoreType.DMA((LOADS,)),
@@ -467,7 +495,7 @@
             jax.ShapeDtypeStruct((4, 32, 512), BF16),
             jax.ShapeDtypeStruct((3, 512, 256), F32),
         ),
-        in_specs=[anywhere] * 5 + [scalars] * 2 + [anywhere] * 6,
+        in_specs=[far] * 5 + [scalars] * 2 + [far] * 6,
         out_specs=(anywhere, anywhere),
         scratch_shapes=scratch,
         compiler_params=pltpu.CompilerParams(
@@ -479,6 +507,22 @@
         cache_len, accepted, entering, low_feature.reshape(4, 32, 512), mid_feature.reshape(4, 32, 512),
         out_proj, join_weight.reshape(1536, 256), teacher,
     )
+    high, grad = pl.pallas_call(
+        deliver,
+        out_shape=(
+            jax.ShapeDtypeStruct((4, 32, 512), BF16),
+            jax.ShapeDtypeStruct((3, 512, 256), F32),
+        ),
+        in_specs=[anywhere] * 2,
+        out_specs=(anywhere, anywhere),
+        scratch_shapes=[
+            pltpu.VMEM((4, 32, 512), BF16),
+            pltpu.VMEM((3, 512, 256), F32),
+            pltpu.SemaphoreType.DMA((2, 4)),
+        ],
+        compiler_params=pltpu.CompilerParams(vmem_limit_bytes=60 * 2**20),
+        name="deliver",
+    )(high, grad)
     return high.reshape(128, 512), grad
 
 

time: 101 us -> 86 us (0.85); the launches traced: 101 us -> 84.4 us
  Pallas kernels: 96.2 us -> 83.8 us
  local copies, waits for them, and re-layouts: 4.22 us -> 0 us
    pallas_call x1, Pallas kernels: 96.2 us -> 81.4 us  [shards(): pl.pallas_call(kernel, out_shape=(jax.ShapeDtypeStruct((4, 32, 512), BF16...]
    unnamed x2 -> x0, local copies, waits for them, and re-layouts: 4.22 us -> none
    pallas_call x0 -> x1, Pallas kernels: none -> 2.32 us  [shards(): pl.pallas_call(deliver, out_shape=(jax.ShapeDtypeStruct((4, 32, 512), BF1...]
where the time goes in v2:
time: 86 us; the launch traced here: 84.4 us
  Pallas kernels  83.8 us (97%)
    pallas_call x1, Pallas kernels, shards(): pl.pallas_call(kernel, out_shape=(jax.ShapeDtypeStruct((4, 32, 512), BF16...  81.4 us
    pallas_call x1, Pallas kernels, shards(): pl.pallas_call(deliver, out_shape=(jax.ShapeDtypeStruct((4, 32, 512), BF1...  2.32 us

profile of v2, /device:TPU:32, one launch (start us, length us, event | category | flops | bytes accessed | tf_op | source)
XLA Modules:
  0.0 84.4 jit_solution(13376541769391726158)
XLA Ops:
  0.6 81.4 %verify_join.1 = (bf16[4,32,512]{2,1,0:T(8,128)(2,1)}, f32[3,512,256]{2,1,0:T(8,128)}) custom-call(bf16[128,512]{1,0:T(8,128)(2,1)} %q_h.1, bf16[128,128]{1,0:T(8,128)(2,1)} %kn_h.1, bf16[128,128]{1,0:T(8,128)(2,1)} %vn_h.1, bf16[4,512,128]{2,1,0:T(8,128)(2,1)} %bitcast.7, bf16[4,512,128]{2,1,0:T(8,128)(2,1)} %bitcast.8, s32[4]{0:T(128)} %clen.1, s32[4]{0:T(128)} %acc.1, ...), custom_call_target="tpu_custom_call" | custom-call | tf_op jit(solution)/shard_map/verify_join/pallas_call | solution.py:492
  82.1 2.3 %deliver.1 = (bf16[4,32,512]{2,1,0:T(8,128)(2,1)}, f32[3,512,256]{2,1,0:T(8,128)}) custom-call(bf16[4,32,512]{2,1,0:T(8,128)(2,1)} %get-tuple-element.6.high_i, f32[3,512,256]{2,1,0:T(8,128)} %get-tuple-element.7.grad_i), custom_call_target="tpu_custom_call" | custom-call | tf_op jit(solution)/shard_map/deliver/pallas_call | solution.py:510

commit v3 on v2

--- a/solution.py
+++ b/solution.py
@@ -8,7 +8,7 @@
 MESH = pl.DeviceIdType.MESH
 F32 = jnp.float32
 BF16 = jnp.bfloat16
-COPIES = 160
+COPIES = 192
 LOADS = 96
 OTHER = {1: 3, 3: 1}
 
@@ -68,7 +68,7 @@
 def kernel(
     q_h, kn_h, vn_h, ck_h, cv_h, clen, acc, ent_h, low_h, mid_h, wo_h, w_h, teach_h,
     high_o, grad_o,
-    q_v, kn_v, vn_v, ck_v, cv_v, ent_v, wo_v, wy, flm, fh, ft, sb, sr, tb, att, joint, xs, xr, zk, zs, zr, es, gath,
+    q_v, kn_v, vn_v, ck_v, cv_v, ent_v, wo_v, wy, flm, fh, ft, sr, tb, att, joint, xs, xr, zk, zs, zr, es, gath,
     grad_v, part1,
     ssem, rsem, lsem,
 ):
@@ -103,10 +103,20 @@
         return copy
 
     barrier = pltpu.get_barrier_semaphore()
-    peers = [dict(dx=1), dict(dx=2), dict(dx=3), dict(dz=1), dict(dz=2), dict(dz=3), dict(dy=1), dict(dy=2), dict(dy=3),
+    peers = [dict(dx=1), dict(dx=2), dict(dx=3), dict(dz=1), dict(dz=2), dict(dz=3), dict(dy=1), dict(dy=3),
              dict(dzl=1), dict(dc=1), dict(dzl=1, dc=1)]
     for p in peers:
         pl.semaphore_signal(barrier, inc=1, device_id=dev(**p), device_id_type=MESH)
+
+    def error_source(ky):
+        return ((xor4(y, ky) * 4 + zl * 2 + c), y * 4 + x)
+
+    for ky in (1, 2, 3):
+        pl.semaphore_signal(barrier, inc=1, device_id=error_source(ky), device_id_type=MESH)
+
+    @pl.when(zh != y)
+    def _():
+        pl.semaphore_signal(barrier, inc=1, device_id=error_source(0), device_id_type=MESH)
 
     l_att = [load(q_h, q_v), load(kn_h, kn_v), load(ck_h, ck_v), load(vn_h, vn_v), load(cv_h, cv_v)]
     l_w = load(w_h, wy.at[0])
@@ -120,7 +130,7 @@
     total = acc[0] + acc[1] + acc[2] + acc[3]
     scale = 4.0 / jnp.full((32, 128), total, jnp.int32).astype(F32)
     place = lax.broadcasted_iota(jnp.int32, (32, 128), 0)
-    sb[...] = jnp.where(place < jnp.full((32, 128), acc[x], jnp.int32), scale, 0.0)
+    sr[0] = jnp.where(place < jnp.full((32, 128), acc[x], jnp.int32), scale, 0.0)
 
     inv = 128 ** (-0.5)
 
@@ -146,41 +156,19 @@
     for cp in l_att:
         cp.wait()
     attend(0)
-    pl.semaphore_wait(barrier, len(peers))
+    pl.semaphore_wait(barrier, len(peers) + 3 + (xor4(y, zh) + 3) // 4)
     w_y1 = send(w_h, wy.at[1], dev(dy=1))
     w_y3 = send(w_h, wy.at[3], dev(dy=3))
 
-    b1, b0 = zh // 2, zh % 2
-    tpeer = (y * 4 + ((zl + b1) % 2) * 2 + (c + b0) % 2, t)
-    tsrc = []
-    for ky in range(4):
-        col = (xor4(y, ky) * 4 + ((zl + b1) % 2) * 2 + (c + b0) % 2) * 256
-        tsrc.append(teach_h.at[pl.ds(pl.multiple_of(x * 32, 32), 32), pl.ds(pl.multiple_of(col, 256), 256)])
-    base_r, base_l = counts[0], counts[1]
-    counts[0] += 5
-    counts[1] += 5
-
-    def teacher_remote(i):
-        src, dst = (tsrc[i], tb.at[i]) if i < 4 else (sb, sr)
-        return pltpu.make_async_remote_copy(
-            src_ref=src, dst_ref=dst, send_sem=ssem.at[base_r + i], recv_sem=rsem.at[base_r + i],
-            device_id=tpeer, device_id_type=MESH,
-        )
-
-    def teacher_local(i):
-        src, dst = (tsrc[i], tb.at[i]) if i < 4 else (sb, sr)
-        return pltpu.make_async_copy(src, dst, lsem.at[base_l + i])
-
-    @pl.when(zh != 0)
-    def _():
-        for i in range(5):
-            teacher_remote(i).start()
-
-    @pl.when(zh == 0)
-    def _():
-        for i in range(5):
-            teacher_local(i).start()
-
+    near = (dict(), dict(dc=1), dict(dzl=1), dict(dzl=1, dc=1))
+
+    def teacher_block(j):
+        col = (zh * 4 + ((zl + j // 2) % 2) * 2 + (c + j % 2) % 2) * 256
+        return teach_h.at[pl.ds(pl.multiple_of(x * 32, 32), 32), pl.ds(pl.multiple_of(col, 256), 256)]
+
+    l_t = load(teacher_block(0), tb.at[0])
+    got_t = [send(teacher_block(j), tb.at[j], dev(**near[j])) for j in (1, 2, 3)]
+    got_t += [send(sr.at[0], sr.at[j], dev(**near[j])) for j in (1, 2, 3)]
     for cp in l_f:
         cp.wait()
     lm_zl = send(flm.at[c, y, zl], flm.at[c, y, zl], dev(dzl=1))
@@ -272,7 +260,7 @@
     for j, (cc, ll) in enumerate(groups):
         rows = jnp.concatenate([flm[cc, y, ll, f].reshape(128, 512) for f in range(2)], axis=1)
         for ky in range(4):
-            joint[j, :, :, ky * 256 : ky * 256 + 256] = dot(rows, wy[ky, 0:1024]).reshape(4, 32, 256)
+            joint[j, :, ky] = dot(rows, wy[ky, 0:1024]).reshape(4, 32, 256)
     l_ent.wait()
     for p, cp, (start, size) in zip(parts, c4, ROW_PARTS):
         value = final(p, cp)
@@ -283,158 +271,171 @@
     h_c = send(fh.at[c, y, zl], fh.at[c, y, zl], dev(dc=1))
     o_high = load(fh.at[c, y, zl], high_o)
 
-    to_x = [None] * 4
+    own_ky = xor4(y, zh)
+    to_x, to_x2 = [None] * 4, [None] * 4
 
     def join(j):
         cc, ll = groups[j]
         rows = fh[cc, y, ll].reshape(128, 512)
         for ky in range(4):
-            cols = slice(ky * 256, ky * 256 + 256)
-            value = joint[j, :, :, cols] + dot(rows, wy[ky, 1024:1536]).reshape(4, 32, 256)
-            joint[j, :, :, cols] = value
-            xs[j, :, :, cols] = value.astype(BF16)
+            value = joint[j, :, ky] + dot(rows, wy[ky, 1024:1536]).reshape(4, 32, 256)
+            joint[j, :, ky] = value
+            xs[j, :, ky] = value.astype(BF16)
         to_x[j] = [send(xs.at[j, xor4(x, k)], xr.at[j, k], dev(dx=k)) for k in (2, 1, 3)]
 
-    base_z = counts[0]
-    counts[0] += 8
-
-    def to_z(j):
-        k = xor4(zh, j)
-        return pltpu.make_async_remote_copy(
-            src_ref=zs.at[j], dst_ref=zr.at[k], send_sem=ssem.at[base_z + j], recv_sem=rsem.at[base_z + 4 + k],
-            device_id=(g, j * 4 + x), device_id_type=MESH,
-        )
+    to_z = [None] * 4
 
     def sum_x(j):
+        for cp in to_x[j]:
+            cp.wait_recv()
         value = joint[j, x]
-        for cp, k in zip(to_x[j], (2, 1, 3)):
-            cp.wait_recv()
         for k in (1, 2, 3):
             value = value + xr[j, k].astype(F32)
         zk[j] = value
         zs[j] = value.astype(BF16)
-
-        @pl.when(zh != j)
+        to_z[j] = [send(zs.at[j, xor4(own_ky, k)], zr.at[j, k], dev(dz=k)) for k in (2, 1, 3)]
+
+    base_e = counts[0]
+    counts[0] += 32
+
+    def error_copy(j, kz, ky):
+        return pltpu.make_async_remote_copy(
+            src_ref=es.at[j], dst_ref=gath.at[j, 0, ky],
+            send_sem=ssem.at[base_e + j * 4 + kz], recv_sem=rsem.at[base_e + 16 + j * 4 + ky],
+            device_id=(zh * 4 + zl * 2 + c, xor4(zh, kz) * 4 + x), device_id_type=MESH,
+        )
+
+    def error(j):
+        for cp in to_z[j]:
+            cp.wait_recv()
+        value = zk[j, own_ky]
+        for k in (1, 2, 3):
+            value = value + zr[j, k].astype(F32)
+        row_scale = jnp.concatenate([sr[j], sr[j]], axis=1)
+        err = ((value - tb[j].astype(F32)) * row_scale).astype(BF16)
+        es[j] = err
+        for kz in (2, 1, 3):
+            error_copy(j, kz, own_ky).start()
+
+        @pl.when(zh != y)
         def _():
-            to_z(j).start()
-
+            error_copy(j, 0, own_ky).start()
+
+        @pl.when(zh == y)
+        def _():
+            gath[j, 0, 0] = es[j]
+
+    def spread(j):
+        for ky in (1, 3, 2):
+            error_copy(j, 0, ky).wait_recv()
+
+        @pl.when(zh != y)
+        def _():
+            error_copy(j, 0, 0).wait_recv()
+
+        to_x2[j] = [send(gath.at[j, 0], gath.at[j, k], dev(dx=k)) for k in (2, 1, 3)]
+
+    def turn(lo, hi, feature):
+        def body(i, carry):
+            j, s = i // 4, xor4(x, i % 4)
+            cc, ll = (c + j % 2) % 2, (zl + j // 2) % 2
+            if feature < 2:
+                blocks = [flm[cc, xor4(y, ky), ll, feature, s] for ky in range(4)]
+            else:
+                blocks = [fh[cc, xor4(y, ky), ll, s] for ky in range(4)]
+            rows = jnp.concatenate(blocks, axis=0)
+            ft[feature, :, pl.ds(pl.multiple_of(i * 128, 128), 128)] = rows.T
+            return carry
+
+        lax.fori_loop(lo, hi, body, 0)
+
+    y1, y3, y2 = xor4(y, 1), xor4(y, 3), xor4(y, 2)
     join(0)
     h_c.wait_recv()
     join(1)
     h_zl.wait_recv()
     h_c2 = send(fh.at[c, y, (zl + 1) % 2], fh.at[c, y, (zl + 1) % 2], dev(dc=1))
     join(2)
+    h_y1 = send(fh.at[c, y], fh.at[c, y], dev(dy=1))
+    h_y3 = send(fh.at[c, y], fh.at[c, y], dev(dy=3))
     sum_x(0)
+    sum_x(1)
     h_c2.wait_recv()
     join(3)
-    h_y1 = send(fh.at[c, y], fh.at[c, y], dev(dy=1))
-    h_y3 = send(fh.at[c, y], fh.at[c, y], dev(dy=3))
-    sum_x(1)
+    l_t.wait()
+    for cp in got_t:
+        cp.wait_recv()
+    error(0)
     sum_x(2)
-    sum_x(3)
-
-    y1, y3, y2 = xor4(y, 1), xor4(y, 3), xor4(y, 2)
+    error(1)
     lm_y1.wait_recv()
     lm_2a = send(flm.at[c, y1, 0], flm.at[c, y1, 0], dev(dy=3))
     lm_y3.wait_recv()
     lm_2b = send(flm.at[c, y3, 1], flm.at[c, y3, 1], dev(dy=1))
+    sum_x(3)
     lm_f = [send(flm.at[c, y1], flm.at[c, y1], dev(dc=1)), send(flm.at[c, y3], flm.at[c, y3], dev(dc=1))]
-
-    def turn(lo, hi, feature):
-        def body(j, carry):
-            kz, kx = j // 4, j % 4
-            zz = xor4(zh, kz)
-            cc, ll = (c + zz % 2) % 2, (zl + zz // 2) % 2
-            s = xor4(x, kx)
-            if feature < 2:
-                blocks = [flm[cc, xor4(y, ky), ll, feature, s] for ky in range(4)]
-            else:
-                blocks = [fh[cc, xor4(y, ky), ll, s] for ky in range(4)]
-            rows = jnp.concatenate(blocks, axis=0)
-            ft[feature, :, pl.ds(pl.multiple_of(j * 128, 128), 128)] = rows.T
-            return carry
-
-        lax.fori_loop(lo, hi, body, 0)
-
-    @pl.when(zh != 0)
-    def _():
-        for i in range(5):
-            teacher_remote(i).wait()
-
-    @pl.when(zh == 0)
-    def _():
-        for i in range(5):
-            teacher_local(i).wait()
-
-    value = zk[zh]
-    for k in (1, 3, 2):
-        pltpu.make_async_remote_copy(
-            src_ref=zs.at[0], dst_ref=zr.at[k], send_sem=ssem.at[base_z], recv_sem=rsem.at[base_z + 4 + k],
-            device_id=dev(dz=k), device_id_type=MESH,
-        ).wait_recv()
-        value = value + zr[k].astype(F32)
-    row_scale = jnp.concatenate([sr[...], sr[...]], axis=1)
-    for ky in (1, 3, 2, 0):
-        err = (value[:, ky * 256 : ky * 256 + 256] - tb[ky].astype(F32)) * row_scale
-        if ky:
-            es[ky] = err.astype(BF16)
-        else:
-            gath[0, 0, 0] = err.astype(BF16)
-    e_y = [send(es.at[ky], gath.at[0, 0, ky], dev(dy=ky)) for ky in (1, 3, 2)]
-    e_z0 = {k: send(gath.at[0, 0, 0], gath.at[k, 0, 0], dev(dz=k)) for k in (2, 1, 3)}
-    for cp in e_y:
-        cp.wait_recv()
-    rest = pl.ds(1, 3)
-    e_z1 = {k: send(gath.at[0, 0, rest], gath.at[k, 0, rest], dev(dz=k)) for k in (2, 1, 3)}
-    e_x = {0: [send(gath.at[0, 0], gath.at[0, k], dev(dx=k)) for k in (2, 1, 3)]}
+    spread(0)
+    error(2)
+    spread(1)
+    error(3)
     h_y1.wait_recv()
     h_2a = send(fh.at[c, y1, 0], fh.at[c, y1, 0], dev(dy=3))
     h_y3.wait_recv()
     h_2b = send(fh.at[c, y3, 1], fh.at[c, y3, 1], dev(dy=1))
     h_f = [send(fh.at[c, y1], fh.at[c, y1], dev(dc=1)), send(fh.at[c, y3], fh.at[c, y3], dev(dc=1))]
+    spread(2)
     lm_2a.wait_recv()
     lm_2b.wait_recv()
     lm_f.append(send(flm.at[c, y2], flm.at[c, y2], dev(dc=1)))
-    for k in (1, 3):
-        e_z0[k].wait_recv()
-        e_z1[k].wait_recv()
-        e_x[k] = [send(gath.at[k, 0], gath.at[k, q], dev(dx=q)) for q in (2, 1, 3)]
-    e_z0[2].wait_recv()
-    e_z1[2].wait_recv()
-    e_x[2] = [send(gath.at[2, 0], gath.at[2, q], dev(dx=q)) for q in (2, 1, 3)]
+    spread(3)
+    for f in (0, 1):
+        turn(0, 4, f)
+        turn(8, 12, f)
     h_2a.wait_recv()
     h_2b.wait_recv()
     h_f.append(send(fh.at[c, y2], fh.at[c, y2], dev(dc=1)))
     for cp in lm_f:
         cp.wait_recv()
-    turn(0, 16, 0)
-    turn(0, 16, 1)
+    for f in (0, 1):
+        turn(4, 8, f)
+        turn(12, 16, f)
+    outs = []
+
+    def grow(j):
+        for cp in to_x2[j]:
+            cp.wait_recv()
+        block = gath[j].reshape(512, 256)
+        for f in range(3):
+            value = dot(ft[f, :, j * 512 : j * 512 + 512], block)
+            if j:
+                value = grad_v[f] + value
+            grad_v[f] = value
+            if j == 3:
+                outs.append(load(grad_v.at[f], grad_o.at[f]))
+
+    turn(0, 4, 2)
+    grow(0)
+    turn(8, 12, 2)
+    grow(2)
     for cp in h_f:
         cp.wait_recv()
-    turn(0, 16, 2)
-
-    outs = []
-    for k in (0, 1, 3, 2):
-        for cp in e_x[k]:
-            cp.wait_recv()
-        block = gath[k].reshape(512, 256)
-        for f in range(3):
-            value = dot(ft[f, :, k * 512 : k * 512 + 512], block)
-            if k:
-                value = grad_v[f] + value
-            grad_v[f] = value
-            if k == 2:
-                outs.append(load(grad_v.at[f], grad_o.at[f]))
+    turn(4, 8, 2)
+    grow(1)
+    turn(12, 16, 2)
+    grow(3)
     for cp in outs:
         cp.wait()
     o_high.wait()
     for cp in sent:
         cp.wait_send()
     for j in range(4):
-
-        @pl.when(zh != j)
-        def _():
-            to_z(j).wait_send()
+        for kz in (1, 2, 3):
+            error_copy(j, kz, own_ky).wait_send()
+
+    @pl.when(zh != y)
+    def _():
+        for j in range(4):
+            error_copy(j, 0, own_ky).wait_send()
 
 
 def deliver(high_i, grad_i, high_o, grad_o, high_v, grad_v, sem):
@@ -471,16 +472,15 @@
         pltpu.VMEM((2, 4, 2, 2, 4, 32, 512), BF16),
         pltpu.VMEM((2, 4, 2, 4, 32, 512), BF16),
         pltpu.VMEM((3, 512, 2048), BF16),
-        pltpu.VMEM((32, 128), F32),
-        pltpu.VMEM((32, 128), F32),
+        pltpu.VMEM((4, 32, 128), F32),
         pltpu.VMEM((4, 32, 256), BF16),
         pltpu.VMEM((128, 512), BF16),
-        pltpu.VMEM((4, 4, 32, 1024), F32),
-        pltpu.VMEM((4, 4, 32, 1024), BF16),
-        pltpu.VMEM((4, 4, 32, 1024), BF16),
-        pltpu.VMEM((4, 32, 1024), F32),
-        pltpu.VMEM((4, 32, 1024), BF16),
-        pltpu.VMEM((4, 32, 1024), BF16),
+        pltpu.VMEM((4, 4, 4, 32, 256), F32),
+        pltpu.VMEM((4, 4, 4, 32, 256), BF16),
+        pltpu.VMEM((4, 4, 4, 32, 256), BF16),
+        pltpu.VMEM((4, 4, 32, 256), F32),
+        pltpu.VMEM((4, 4, 32, 256), BF16),
+        pltpu.VMEM((4, 4, 32, 256), BF16),
         pltpu.VMEM((4, 32, 256), BF16),
         pltpu.VMEM((4, 4, 4, 32, 256), BF16),
         pltpu.VMEM((3, 512, 256), F32),

time: 86 us -> 82.4 us (0.958)
  Pallas kernels: 83.8 us -> 80.1 us
    pallas_call x1, Pallas kernels: 81.4 us -> 77.8 us  [shards(): pl.pallas_call(kernel, out_shape=(jax.ShapeDtypeStruct((4, 32, 512), BF16...]
where the time goes in v3:
time: 82.4 us; the launch traced here: 80.8 us
  Pallas kernels  80.1 us (97%)
    pallas_call x1, Pallas kernels, shards(): pl.pallas_call(kernel, out_shape=(jax.ShapeDtypeStruct((4, 32, 512), BF16...  77.8 us
    pallas_call x1, Pallas kernels, shards(): pl.pallas_call(deliver, out_shape=(jax.ShapeDtypeStruct((4, 32, 512), BF1...  2.32 us

profile of v3, /device:TPU:32, one launch (start us, length us, event | category | flops | bytes accessed | tf_op | source)
XLA Modules:
  0.0 80.8 jit_solution(9652339759213198785)
XLA Ops:
  0.6 77.8 %verify_join.1 = (bf16[4,32,512]{2,1,0:T(8,128)(2,1)}, f32[3,512,256]{2,1,0:T(8,128)}) custom-call(bf16[128,512]{1,0:T(8,128)(2,1)} %q_h.1, bf16[128,128]{1,0:T(8,128)(2,1)} %kn_h.1, bf16[128,128]{1,0:T(8,128)(2,1)} %vn_h.1, bf16[4,512,128]{2,1,0:T(8,128)(2,1)} %bitcast.7, bf16[4,512,128]{2,1,0:T(8,128)(2,1)} %bitcast.8, s32[4]{0:T(128)} %clen.1, s32[4]{0:T(128)} %acc.1, ...), custom_call_target="tpu_custom_call" | custom-call | tf_op jit(solution)/shard_map/verify_join/pallas_call | solution.py:492
  78.4 2.3 %deliver.1 = (bf16[4,32,512]{2,1,0:T(8,128)(2,1)}, f32[3,512,256]{2,1,0:T(8,128)}) custom-call(bf16[4,32,512]{2,1,0:T(8,128)(2,1)} %get-tuple-element.6.high_i, f32[3,512,256]{2,1,0:T(8,128)} %get-tuple-element.7.grad_i), custom_call_target="tpu_custom_call" | custom-call | tf_op jit(solution)/shard_map/deliver/pallas_call | solution.py:510

commit v4 on v3

--- a/solution.py
+++ b/solution.py
@@ -132,6 +132,9 @@
     place = lax.broadcasted_iota(jnp.int32, (32, 128), 0)
     sr[0] = jnp.where(place < jnp.full((32, 128), acc[x], jnp.int32), scale, 0.0)
 
+    pl.semaphore_wait(barrier, len(peers) + 3 + (xor4(y, zh) + 3) // 4)
+    w_y1 = send(w_h, wy.at[1], dev(dy=1))
+    w_y3 = send(w_h, wy.at[3], dev(dy=3))
     inv = 128 ** (-0.5)
 
     def attend(s):
@@ -156,9 +159,6 @@
     for cp in l_att:
         cp.wait()
     attend(0)
-    pl.semaphore_wait(barrier, len(peers) + 3 + (xor4(y, zh) + 3) // 4)
-    w_y1 = send(w_h, wy.at[1], dev(dy=1))
-    w_y3 = send(w_h, wy.at[3], dev(dy=3))
 
     near = (dict(), dict(dc=1), dict(dzl=1), dict(dzl=1, dc=1))
 
@@ -355,9 +355,9 @@
     join(1)
     h_zl.wait_recv()
     h_c2 = send(fh.at[c, y, (zl + 1) % 2], fh.at[c, y, (zl + 1) % 2], dev(dc=1))
-    join(2)
     h_y1 = send(fh.at[c, y], fh.at[c, y], dev(dy=1))
     h_y3 = send(fh.at[c, y], fh.at[c, y], dev(dy=3))
+    join(2)
     sum_x(0)
     sum_x(1)
     h_c2.wait_recv()

time: 82.4 us -> 82.1 us (level)
  no operation moved by 1% of the time
where the time goes in v4:
time: 82.1 us; the launch traced here: 80.8 us
  Pallas kernels  80.2 us (98%)
    pallas_call x1, Pallas kernels, shards(): pl.pallas_call(kernel, out_shape=(jax.ShapeDtypeStruct((4, 32, 512), BF16...  77.9 us
    pallas_call x1, Pallas kernels, shards(): pl.pallas_call(deliver, out_shape=(jax.ShapeDtypeStruct((4, 32, 512), BF1...  2.32 us

profile of v4, /device:TPU:32, one launch (start us, length us, event | category | flops | bytes accessed | tf_op | source)
XLA Modules:
  0.0 80.8 jit_solution(13254544588989193529)
XLA Ops:
  0.6 77.9 %verify_join.1 = (bf16[4,32,512]{2,1,0:T(8,128)(2,1)}, f32[3,512,256]{2,1,0:T(8,128)}) custom-call(bf16[128,512]{1,0:T(8,128)(2,1)} %q_h.1, bf16[128,128]{1,0:T(8,128)(2,1)} %kn_h.1, bf16[128,128]{1,0:T(8,128)(2,1)} %vn_h.1, bf16[4,512,128]{2,1,0:T(8,128)(2,1)} %bitcast.7, bf16[4,512,128]{2,1,0:T(8,128)(2,1)} %bitcast.8, s32[4]{0:T(128)} %clen.1, s32[4]{0:T(128)} %acc.1, ...), custom_call_target="tpu_custom_call" | custom-call | tf_op jit(solution)/shard_map/verify_join/pallas_call | solution.py:492
  78.5 2.3 %deliver.1 = (bf16[4,32,512]{2,1,0:T(8,128)(2,1)}, f32[3,512,256]{2,1,0:T(8,128)}) custom-call(bf16[4,32,512]{2,1,0:T(8,128)(2,1)} %get-tuple-element.6.high_i, f32[3,512,256]{2,1,0:T(8,128)} %get-tuple-element.7.grad_i), custom_call_target="tpu_custom_call" | custom-call | tf_op jit(solution)/shard_map/deliver/pallas_call | solution.py:510
